TPU v7x, 32 devices: a whole 2x2x4 slice. The times are simulated.
32 devices in a mesh: gx: 4 (over y, x), gz: 2 (over core), gy: 4 (over z).
Axes of the slice: x: 2, y: 2, z: 4, core: 2. Of those that a mesh axis runs over, the one named last changes fastest.
Arguments:
- fields: bfloat16 [1, 256, 1024, 2048], P(None, 'gy', 'gz', 'gx'), may hold values from -6 to 6
- conductance: float32 [257], replicated, may hold values from 0.5 to 2
- metric: float32 [256], replicated, may hold values from 0.5 to 2
- section_shift: float32 [256], replicated, may hold values from 0.002 to 0.02
- curvature: float32 [256], replicated, may hold values from 0.005 to 0.05
- damping: float32 [1], replicated, may hold values from 0.002 to 0.02
Outputs:
- adjoint_modes: float32 [1, 256, 512, 1024], P(None, 'gy', ('gx', 'gz'))
All inputs are finite; a program needn't handle non-finite values.
Results may differ from a plain program's by a relative error of at most 0.0003.
Values may be sent and summed in bfloat16 or wider, within the bound.
A program may use at most 256 MiB of HBM per device.

v0:
```python
import math

import jax
import jax.numpy as jnp
from jax import lax
from jax.sharding import PartitionSpec as P

TWO_PI = 2.0 * math.pi
PRECISE = lax.Precision.HIGH


def prefix_2(part, axis, combine, identity, reverse):
    count = lax.axis_size(axis)
    place = lax.axis_index(axis)
    ahead = count - 1 - place if reverse else place
    gathered = jax.tree.map(lambda a: lax.all_gather(a, axis), part)
    state = jax.tree.map(lambda a, e: jnp.zeros_like(a) + jnp.asarray(e, a.dtype), part, identity)

    def one(hop, state):
        source = count - 1 - hop if reverse else hop
        return combine(
            state, jax.tree.map(lambda a: lax.dynamic_index_in_dim(a, source, 0, False), gathered)
        )

    return lax.fori_loop(0, ahead, one, state)


def wave_square(along_first, along_local, along_total, across_total):
    along = (along_first + jnp.arange(along_local, dtype=jnp.int32)).astype(
        jnp.float32
    ) / along_total
    index = jnp.arange(2 * across_total, dtype=jnp.int32) % across_total
    signed = jnp.where(index < across_total // 2, index, index - across_total)
    across = signed.astype(jnp.float32) / (across_total // 2)
    return along[:, None] * along[:, None] + across[None, :] * across[None, :]


def forward_compose(earlier, later):
    return (
        later[0] * earlier[0] + later[1] * earlier[5],
        later[0] * earlier[1] + later[1] * earlier[6],
        later[2] * earlier[0] + later[3] * earlier[2] + later[4] * earlier[5],
        later[3] * earlier[3],
        later[2] * earlier[1] + later[3] * earlier[4] + later[4] * earlier[6],
        later[5] * earlier[0] + later[6] * earlier[5],
        later[5] * earlier[1] + later[6] * earlier[6],
    )


def backward_compose(earlier, later):
    return (later[0] - later[1] * earlier[0], -later[1] * earlier[1])


def local(fields, conductance, metric, section_shift, curvature, damping):
    components, row_count = (fields.shape[0], fields.shape[1])
    along_groups = lax.axis_size("gx")
    across_groups = lax.axis_size("gz")
    joint_groups = along_groups * across_groups
    my_group = lax.axis_index("gy")
    pencils = lax.all_to_all(fields, "gx", split_axis=2, concat_axis=3, tiled=True)
    z_local, along_length = (pencils.shape[2], pencils.shape[3])
    along_total = along_length // 4
    along_local = along_total // joint_groups
    positions = jnp.arange(along_length, dtype=jnp.int32)
    numbers = jnp.arange(along_total, dtype=jnp.int32)
    angles = (positions[:, None] * numbers[None, :] % along_length).astype(jnp.float32) * (
        TWO_PI / along_length
    )
    norm_along = 1.0 / math.sqrt(along_length)
    cos_along = (jnp.cos(angles) * norm_along).reshape(along_length, joint_groups, along_local)
    sin_along = (-jnp.sin(angles) * norm_along).reshape(along_length, joint_groups, along_local)
    real_along = jnp.einsum(
        "cyzx,xbm->czbym", pencils, cos_along, precision=PRECISE, preferred_element_type=jnp.float32
    )
    imaginary_streamwise = jnp.einsum(
        "cyzx,xbm->czbym", pencils, sin_along, precision=PRECISE, preferred_element_type=jnp.float32
    )
    spectra = jnp.stack([real_along, imaginary_streamwise], axis=3).reshape(
        components, z_local, joint_groups, 2 * row_count * along_local
    )
    across_length = joint_groups * z_local
    zpencil = lax.all_to_all(spectra, ("gx", "gz"), split_axis=2, concat_axis=1, tiled=True)
    order = jnp.arange(across_length, dtype=jnp.int32)
    sender = order // z_local
    placed = (
        sender % across_groups * (z_local * along_groups)
        + sender // across_groups * z_local
        + order % z_local
    )
    zdata = zpencil.reshape(components, across_length, 2, row_count * along_local)
    across_total = across_length // 2
    kz_width = across_total // 4
    norm_across = 1.0 / math.sqrt(across_length)
    real_parts = []
    imag_parts = []
    for kz_block in range(4):
        index = kz_block * kz_width + jnp.arange(kz_width, dtype=jnp.int32)
        signed = jnp.where(index < across_total // 2, index, index - across_total)
        phases = (placed[:, None] * signed[None, :] % across_length).astype(jnp.float32) * (
            TWO_PI / across_length
        )
        cosine = jnp.cos(phases) * norm_across
        sine = jnp.sin(phases) * norm_across
        real_parts.append(
            jnp.einsum(
                "czpn,pzk->cnk",
                zdata,
                jnp.stack([cosine, sine]),
                precision=PRECISE,
                preferred_element_type=jnp.float32,
            )
        )
        imag_parts.append(
            jnp.einsum(
                "czpn,pzk->cnk",
                zdata,
                jnp.stack([-sine, cosine]),
                precision=PRECISE,
                preferred_element_type=jnp.float32,
            )
        )
    real_across = jnp.concatenate(real_parts, axis=2).reshape(
        components, row_count, along_local, across_total
    )
    imag_across = jnp.concatenate(imag_parts, axis=2).reshape(
        components, row_count, along_local, across_total
    )
    source = jnp.concatenate([real_across, imag_across], axis=3)
    joint_index = lax.axis_index("gx") * across_groups + lax.axis_index("gz")
    square = wave_square(joint_index * along_local, along_local, along_total, across_total)
    first_row = my_group * row_count
    nought_one = jnp.zeros((1,), jnp.float32)
    metric_pad = jnp.concatenate([nought_one, metric, nought_one])
    metric_rows = lax.dynamic_slice_in_dim(metric_pad, first_row, row_count + 2)
    face_rows = lax.dynamic_slice_in_dim(conductance, first_row, row_count + 1)
    shift_rows = lax.dynamic_slice_in_dim(section_shift, first_row, row_count)
    curve_rows = lax.dynamic_slice_in_dim(curvature, first_row, row_count)
    lower_band = -metric_rows[:row_count] * face_rows[:row_count]
    upper_band = -metric_rows[2:] * face_rows[1:]
    diag_base = (
        metric_rows[1 : row_count + 1] * (face_rows[:row_count] + face_rows[1:]) + shift_rows
    )
    diagonals = [
        diag_base[current_row] + damping[:, None, None] + curve_rows[current_row] * square[None]
        for current_row in range(row_count)
    ]
    unity = jnp.ones((components, along_local, 2 * across_total), jnp.float32)
    nought = jnp.zeros_like(unity)
    identity = (unity, nought, nought, unity, nought, nought, unity)
    state = identity
    for current_row in range(row_count):
        row_map = (
            0.0,
            upper_band[current_row],
            0.0,
            -lower_band[current_row],
            source[:, current_row],
            -lower_band[current_row],
            diagonals[current_row],
        )
        state = forward_compose(state, row_map)
    pivot_scale = 1.0 / state[6]
    local_map = tuple((entry * pivot_scale for entry in state))
    prefix = prefix_2(local_map, "gy", forward_compose, identity, False)
    ratios = prefix[1] / prefix[6]
    forward_swept = prefix[4] / prefix[6]
    multiplier_rows = []
    reduced_rows = []
    for current_row in range(row_count):
        pivots = diagonals[current_row] - lower_band[current_row] * ratios
        ratios = upper_band[current_row] / pivots
        forward_swept = (source[:, current_row] - lower_band[current_row] * forward_swept) / pivots
        multiplier_rows.append(ratios)
        reduced_rows.append(forward_swept)
    index_displacement = reduced_rows[-1]
    slopes = multiplier_rows[-1]
    for current_row in range(row_count - 2, -1, -1):
        index_displacement = (
            reduced_rows[current_row] - multiplier_rows[current_row] * index_displacement
        )
        slopes = -multiplier_rows[current_row] * slopes
    beyond = prefix_2((index_displacement, slopes), "gy", backward_compose, (nought, -unity), True)
    following_value = beyond[0]
    solved_rows = [None] * row_count
    for current_row in range(row_count - 1, -1, -1):
        following_value = reduced_rows[current_row] - multiplier_rows[current_row] * following_value
        solved_rows[current_row] = following_value
    return jnp.stack(solved_rows, axis=1)


def solution(mesh):
    placed = (P(None, "gy", "gz", "gx"), P(), P(), P(), P(), P())
    return jax.shard_map(
        local,
        mesh=mesh,
        in_specs=placed,
        out_specs=P(None, "gy", ("gx", "gz"), None),
        check_vma=False,
    )
```

profile of v0, /device:TPU:0, one launch (start us, length us, event | category | flops | bytes accessed | tf_op | source)
XLA Modules:
  0.0 2477.0 jit_solution(4920253176705296238)
XLA Ops:
  6.5 31.1 %copy.37 = bf16[1,64,512,512]{3,1,0,2:T(8,128)(2,1)} copy(bf16[1,64,512,512]{3,2,1,0:T(8,128)(2,1)} %param.10) | data formatting | bytes 67108864 | tf_op args[0]
  83.1 328.1 %all-to-all-done = bf16[1,64,512,512]{3,1,0,2:T(8,128)(2,1)} async-done(((bf16[1,64,512,512]{3,1,0,2:T(8,128)(2,1)}), bf16[1,64,512,512]{3,1,0,2:T(8,128)(2,1)}, u32[]{:S(2)}, u32[]{:S(2)}) %all-to-all-start) | async-done | bytes 33554464 | tf_op jit(solution)/shard_map/all_to_all | solution.py:60
  411.2 42.3 %copy.62 = bf16[1,64,4,128,512]{4,2,3,1,0:T(4,128)(2,1)} copy(bf16[1,64,4,128,512]{4,1,3,2,0:T(8,128)(2,1)} %bitcast.12) | data formatting | bytes 67108864 | tf_op jit(solution)/shard_map/all_to_all | solution.py:60
  453.5 53.9 %reshape.5765 = bf16[64,128,2048,1]{2,1,0,3:T(8,128)(2,1)} reshape(bf16[1,64,128,4,512]{4,3,2,1,0:T(4,128)(2,1)} %bitcast.2467) | data formatting | bytes 67108864 | tf_op jit(solution)/shard_map/reshape
  507.4 42.2 %convolution_bitcast_fusion = f32[1,128,8,1,64,64]{1,5,4,2,3,0:T(8,128)} fusion(bf16[64,128,2048,1]{2,1,0,3:T(8,128)(2,1)} %reshape.5765, f32[2048,8,64,1]{0,2,3,1:T(8,128)} %fusion.1142), kind=kOutput, calls=%fused_computation.15 | convolution fusion | flops 51539607552 | bytes 54525952 | tf_op jit(solution)/shard_map/cyzx,xbm->czbym/dot_general | solution.py:75
  549.6 41.3 %convolution_bitcast_fusion.1 = f32[1,128,8,1,64,64]{1,5,4,2,3,0:T(8,128)} fusion(bf16[64,128,2048,1]{2,1,0,3:T(8,128)(2,1)} %reshape.5765, f32[2048,8,64,1]{0,2,3,1:T(8,128)S(1)} %copy-done.57), kind=kOutput, calls=%fused_computation.16 | convolution fusion | flops 51539607552 | bytes 54525952 | tf_op jit(solution)/shard_map/cyzx,xbm->czbym/dot_general | solution.py:72
  716.5 23.8 multiply_add_fusion.44
  740.3 23.8 multiply_add_fusion.104
  764.2 95.8 %fusion.1055 = (f32[64,1024]{1,0:T(8,128)}, f32[64,1024]{1,0:T(8,128)S(1)}, f32[64,1024]{1,0:T(8,128)S(1)}, f32[64,1024]{1,0:T(8,128)S(1)}, f32[64,1024]{1,0:T(8...) fusion(f32[]{:T(128)} %bitcast.315, ...), kind=kLoop, calls=%fused_computation.1710 | loop fusion | flops 32899072 | bytes 5248248 | tf_op jit(solution)/shard_map/mul | solution.py:163
  859.9 95.6 %fusion.407 = (f32[64,1024]{1,0:T(8,128)}, f32[64,1024]{1,0:T(8,128)S(1)}, f32[64,1024]{1,0:T(8,128)S(1)}, f32[64,1024]{1,0:T(8,128)}, f32[64,1024]{1,0:T(8,128)...) fusion(f32[]{:T(128)} %bitcast.318, ...), kind=kLoop, calls=%fused_computation.592 | loop fusion | flops 32964608 | bytes 5248248 | tf_op jit(solution)/shard_map/mul | solution.py:163
  1150.3 20.7 multiply_add_fusion.47
  1201.6 31.8 %copy.41 = f32[1,8,128,1,8192]{2,1,4,3,0:T(8,128)} copy(f32[1,8,128,1,8192]{2,4,1,3,0:T(8,128)} %bitcast.26) | data formatting | bytes 67108864 | tf_op jit(solution)/shard_map/all_to_all | solution.py:82
  1233.4 35.5 %reshape.5753 = f32[1024,2,4096]{0,2,1:T(8,128)} reshape(f32[1,8,128,1,8192]{2,1,4,3,0:T(8,128)} %copy.41) | data formatting | bytes 67108864 | tf_op jit(solution)/shard_map/reshape.5
  1391.9 21.1 bitcast_dynamic-update-slice_fusion.1
  1433.7 102.6 %fusion.600 = f32[64,1024]{1,0:T(8,128)} fusion(f32[64,1024]{1,0:T(8,128)S(1)} %get-tuple-element.403, f32[64,1024]{1,0:T(8,128)} %get-tuple-element.405, f32[64,1024]{1,0:T(8,128)} %get-tuple-element.407, f32[64,1024]{1,0:T(8,128)} %get-tuple-element.409, f32[64,1024]{1,0:T(8,128)} %get-tuple-element.411, f32[64,1024]{1,0:T(8,128)} %get-tuple-element.413, ...), kind=kLoop, calls=%fused_computation.914 | loop fusion | flops 48103424 | bytes 24157056 | tf_op jit(solution)/shard_map/mul | solution.py:163
  1536.5 101.0 %fusion.602 = f32[64,1024]{1,0:T(8,128)} fusion(f32[64,1024]{1,0:T(8,128)S(1)} %get-tuple-element.386, f32[64,1024]{1,0:T(8,128)S(1)} %copy-done.66, f32[64,1024]{1,0:T(8,128)S(1)} %copy-done.68, f32[64,1024]{1,0:T(8,128)S(1)} %copy-done.70, f32[64,1024]{1,0:T(8,128)} %get-tuple-element.394, f32[64,1024]{1,0:T(8,128)} %get-tuple-element.396, ...), kind=kLoop, calls=%fused_computation.916 | loop fusion | flops 46858240 | bytes 23894912 | tf_op jit(solution)/shard_map/mul | solution.py:163
  1637.7 29.7 %all-gather.27.cloned.1.call-done = f32[256,1024]{1,0:T(8,128)} async-done(((f32[64,1024]{1,0:T(8,128)}), f32[256,1024]{1,0:T(8,128)}) %all-gather.27.cloned.1.call-update) | async-done | bytes 1048592 | tf_op jit(solution)/shard_map/all_gather | solution.py:16
  1668.4 40.9 %fusion.989 = (f32[1,64,1024]{2,1,0:T(8,128)S(1)}, f32[1,64,1024]{2,1,0:T(8,128)S(1)}, f32[1,64,1024]{2,1,0:T(8,128)S(1)}, f32[1,64,1024]{2,1,0:T(8,128)S(1)}, f...) fusion(f32[]{:T(128)} %bitcast.140, f32[]{:T(128)} %bitcast.147, f32[]{:T(128)} %bitcast.146, f32[]{:T(128)} %bitcast.145, ...), kind=kLoop, calls=%fused_computation.1613 | loop fusion | flops 7012352 | bytes 2101840 | tf_op jit(solution)/shard_map/div | solution.py:171
  1709.3 115.1 %multiply_multiply_fusion = (f32[1,64,1024]{2,1,0:T(8,128)}, f32[1,64,1024]{2,1,0:T(8,128)S(1)}, f32[1,64,1024]{2,1,0:T(8,128)S(1)}, f32[1,64,1024]{2,1,0:T(8,12...) fusion(f32[1,64,1024]{2,1,0:T(8,128)S(1)} %get-tuple-element.37, ...), kind=kLoop, calls=%fused_computation.1446 | loop fusion | flops 27328512 | bytes 4199584 | tf_op jit(solution)/shard_map/mul | solution.py:181
  1824.5 138.0 %fusion.539 = (f32[1,64,1024]{2,1,0:T(8,128)S(1)}, f32[1,64,1024]{2,1,0:T(8,128)S(1)}, f32[1,64,1024]{2,1,0:T(8,128)S(1)}, f32[1,64,1024]{2,1,0:T(8,128)S(1)}, f...) fusion(f32[1,64,64,1024]{3,2,1,0:T(8,128)} %bitcast_dynamic-upd, ...), kind=kLoop, calls=%fused_computation.792 | loop fusion | flops 31129600 | bytes 27268240 | tf_op jit(solution)/shard_map/div | solution.py:172
  1965.2 113.4 %multiply_subtract_fusion.63 = f32[1,64,1024]{2,1,0:T(8,128)} fusion(f32[1,64,1024]{2,1,0:T(8,128)S(1)} %get-tuple-element.376, f32[1,64,1024]{2,1,0:T(8,128)S(1)} %get-tuple-element.382, f32[1,64,1024]{2,1,0:T(8,128)S(1)} %get-tuple-element.375, f32[1,64,1024]{2,1,0:T(8,128)S(1)} %get-tuple-element.374, f32[1,64,1024]{2,1,0:T(8,128)S(1)} %get-tuple-element.381, ...), kind=kLoop, calls=%fused_computation.1447 | loop fusion | flops 31981568 | bytes 20976652 | tf_op jit(solution)/shard_map/sub | solution.py:179
  2079.4 32.1 %all-gather.33.cloned.1.call-done = f32[4,64,1024]{2,1,0:T(8,128)} async-done(((f32[1,64,1024]{2,1,0:T(8,128)}), f32[4,64,1024]{2,1,0:T(8,128)}) %all-gather.33.cloned.1.call-update) | async-done | bytes 1048592 | tf_op jit(solution)/shard_map/all_gather | solution.py:16
  2111.4 29.0 %all-gather.35.cloned.1.call-done = f32[4,64,1024]{2,1,0:T(8,128)} async-done(((f32[1,64,1024]{2,1,0:T(8,128)}), f32[4,64,1024]{2,1,0:T(8,128)}) %all-gather.35.cloned.1.call-update) | async-done | bytes 1048592 | tf_op jit(solution)/shard_map/all_gather | solution.py:16
  2159.4 97.6 %bitcast_dynamic-update-slice_fusion.71 = (f32[1,64,64,1024]{3,2,1,0:T(8,128)}, f32[1,64,1024]{2,1,0:T(8,128)S(1)}, f32[1,64,1024]{2,1,0:T(8,128)S(1)}, f32[1,64...) fusion(f32[1,64,1024]{2,1,0:T(8,128)} %copy-done.55, ...), kind=kLoop, calls=%fused_computation.784 | loop fusion | flops 30212096 | bytes 25695200
  (321 shorter events, 695.5 us)
Async XLA Ops:
  37.6 373.6 %all-to-all-start = ((bf16[1,64,512,512]{3,1,0,2:T(8,128)(2,1)}), bf16[1,64,512,512]{3,1,0,2:T(8,128)(2,1)}, u32[]{:S(2)}, u32[]{:S(2)}) async-start(bf16[1,64,512,512]{3,1,0,2:T(8,128)(2,1)} %copy.37), calls=%async_computation | async-start | bytes 67108864 | tf_op jit(solution)/shard_map/all_to_all | solution.py:60
  614.1 587.6 %all-to-all-start.1 = ((f32[1,128,8,8192]{1,3,0,2:T(8,128)}), f32[1,128,8,8192]{1,3,0,2:T(8,128)}, u32[]{:S(2)}, u32[]{:S(2)}) async-start(f32[1,128,8,8192]{1,3,0,2:T(8,128)} %bitcast.2466), calls=%async_computation.1 | async-start | bytes 67108864 | tf_op jit(solution)/shard_map/all_to_all | solution.py:82
  621.4 1016.2 %all-gather.19.cloned.1.call-start = ((), (), s32[]{:S(2)}) async-start(), calls=%async_computation.2 | async-start | bytes 1310720 | tf_op jit(solution)/shard_map/all_gather | solution.py:16
  740.3 451.2 %copy-start.59 = (f32[64,1024]{1,0:T(8,128)}, f32[64,1024]{1,0:T(8,128)S(1)}, u32[]{:S(2)}) copy-start(f32[64,1024]{1,0:T(8,128)S(1)} %multiply_add_fusion.44) | copy-start | bytes 786436
  764.2 427.3 %copy-start.61 = (f32[64,1024]{1,0:T(8,128)}, f32[64,1024]{1,0:T(8,128)S(1)}, u32[]{:S(2)}) copy-start(f32[64,1024]{1,0:T(8,128)S(1)} %multiply_add_fusion.104) | copy-start | bytes 786436
  962.3 675.3 %all-gather.21.cloned.1.call-start = ((), (), s32[]{:S(2)}) async-start(), calls=%async_computation.3 | async-start | bytes 1310720 | tf_op jit(solution)/shard_map/all_gather | solution.py:16
  969.1 668.5 %all-gather.25.cloned.1.call-start = ((), (), s32[]{:S(2)}) async-start(), calls=%async_computation.5 | async-start | bytes 1310720 | tf_op jit(solution)/shard_map/all_gather | solution.py:16
  971.4 666.2 %all-gather.29.cloned.1.call-start = ((), (), s32[]{:S(2)}) async-start(), calls=%async_computation.7 | async-start | bytes 1310720 | tf_op jit(solution)/shard_map/all_gather | solution.py:16
  972.0 665.7 %all-gather.31.cloned.1.call-start = ((), (), s32[]{:S(2)}) async-start(), calls=%async_computation.8 | async-start | bytes 1310720 | tf_op jit(solution)/shard_map/all_gather | solution.py:16
  972.6 665.1 %all-gather.23.cloned.1.call-start = ((), (), s32[]{:S(2)}) async-start(), calls=%async_computation.4 | async-start | bytes 1310720 | tf_op jit(solution)/shard_map/all_gather | solution.py:16
  1536.4 131.1 %all-gather.27.cloned.1.call-start = ((), (), s32[]{:S(2)}) async-start(), calls=%async_computation.6 | async-start | bytes 1310720 | tf_op jit(solution)/shard_map/all_gather | solution.py:16
  1637.5 473.9 %all-gather.33.cloned.1.call-start = ((), (), s32[]{:S(2)}) async-start(), calls=%async_computation.9 | async-start | bytes 1310720 | tf_op jit(solution)/shard_map/all_gather | solution.py:16
  1668.4 296.8 %slice-start = ((s8[16777216]{0:T(1024)(128)(4,1)}), s8[4194304]{0:T(1024)(128)(4,1)S(1)}, s32[]{:S(2)}) async-start(s8[16777216]{0:T(1024)(128)(4,1)} %bitcast.2462), calls=%async_computation.11 | async-start | bytes 8388608
  1709.3 253.4 %copy-start = (f32[1,64,1024]{2,1,0:T(8,128)}, f32[1,64,1024]{2,1,0:T(8,128)S(1)}, u32[]{:S(2)}) copy-start(f32[1,64,1024]{2,1,0:T(8,128)S(1)} %get-tuple-element.379) | copy-start | bytes 786436
  1824.4 138.3 %copy-start.7 = (f32[1,64,1024]{2,1,0:T(8,128)}, f32[1,64,1024]{2,1,0:T(8,128)S(1)}, u32[]{:S(2)}) copy-start(f32[1,64,1024]{2,1,0:T(8,128)S(1)} %get-tuple-element.348) | copy-start | bytes 786436
  1824.4 138.4 %copy-start.9 = (f32[1,64,1024]{2,1,0:T(8,128)}, f32[1,64,1024]{2,1,0:T(8,128)S(1)}, u32[]{:S(2)}) copy-start(f32[1,64,1024]{2,1,0:T(8,128)S(1)} %get-tuple-element.350) | copy-start | bytes 786436
  1824.4 140.7 %slice-start.1 = ((s8[16777216]{0:T(1024)(128)(4,1)}), s8[4194304]{0:T(1024)(128)(4,1)S(1)}, s32[]{:S(2)}) async-start(s8[16777216]{0:T(1024)(128)(4,1)} %bitcast.2462), calls=%async_computation.12 | async-start | bytes 8388608
  1824.5 140.7 %slice-start.2 = ((s8[16777216]{0:T(1024)(128)(4,1)}), s8[4194304]{0:T(1024)(128)(4,1)S(1)}, s32[]{:S(2)}) async-start(s8[16777216]{0:T(1024)(128)(4,1)} %bitcast.2462), calls=%async_computation.13 | async-start | bytes 8388608
  1824.5 140.7 %slice-start.3 = ((s8[16777216]{0:T(1024)(128)(4,1)}), s8[4194304]{0:T(1024)(128)(4,1)S(1)}, s32[]{:S(2)}) async-start(s8[16777216]{0:T(1024)(128)(4,1)} %bitcast.2462), calls=%async_computation.14 | async-start | bytes 8388608
  2078.6 61.8 %all-gather.35.cloned.1.call-start = ((), (), s32[]{:S(2)}) async-start(), calls=%async_computation.10 | async-start | bytes 1310720 | tf_op jit(solution)/shard_map/all_gather | solution.py:16
  2159.4 145.7 %copy-start.26 = (f32[1,64,1024]{2,1,0:T(8,128)S(1)}, f32[1,64,1024]{2,1,0:T(8,128)}, u32[]{:S(2)}) copy-start(f32[1,64,1024]{2,1,0:T(8,128)} %copy-done.25) | copy-start | bytes 786436
  2159.4 145.7 %copy-start.54 = (f32[1,64,1024]{2,1,0:T(8,128)S(1)}, f32[1,64,1024]{2,1,0:T(8,128)}, u32[]{:S(2)}) copy-start(f32[1,64,1024]{2,1,0:T(8,128)} %copy-done.53) | copy-start | bytes 786436
  2159.4 160.1 %copy-start.1 = (f32[1,64,1024]{2,1,0:T(8,128)S(1)}, f32[1,64,1024]{2,1,0:T(8,128)}, u32[]{:S(2)}) copy-start(f32[1,64,1024]{2,1,0:T(8,128)} %copy-done) | copy-start | bytes 786436
  2159.4 160.1 %copy-start.52 = (f32[1,64,1024]{2,1,0:T(8,128)S(1)}, f32[1,64,1024]{2,1,0:T(8,128)}, u32[]{:S(2)}) copy-start(f32[1,64,1024]{2,1,0:T(8,128)} %copy-done.51) | copy-start | bytes 786436
  (69 other events, 3766.3 us)
Sparse Core Ops, SparseCore 0:
  962.4 29.7 all-gather.18
  993.8 27.4 all-gather.20
  1022.8 27.4 all-gather.24
  1051.7 27.4 all-gather.28
  1080.6 27.4 all-gather.30
  1536.5 29.6 all-gather.22
  1637.6 29.7 all-gather.26
  2078.8 32.6 all-gather.32
  2113.0 27.4 all-gather.34
where the time goes:
time: 2500 us; the launch traced here: 2480 us
  other arithmetic  1450 us (58%)
  waiting for transfers between devices  421 us (17%)
  matrix products  248 us (10%)
  local copies, waits for them, and re-layouts  237 us (9%)
  between operations  98.6 us (4%)
    mul x7, other arithmetic, local(): local_map = tuple((entry * pivot_scale for entry in state))  409 us
    all_to_all x1, waiting for transfers between devices, local(): lax.all_to_all(fields, 'gx', split_axis=2, concat_axis=3, tiled=True)  328 us
    unnamed x44, other arithmetic  294 us
    div x1, other arithmetic, local(): (source[:, current_row] - lower_band[current_row] * forward_swept) / pivots  138 us
    mul x1, other arithmetic, local(): slopes = -multiplier_rows[current_row] * slopes  115 us
    sub x1, other arithmetic, local(): reduced_rows[current_row]  113 us
    all_gather x9, waiting for transfers between devices, prefix_2(): gathered = jax.tree.map(lambda a: lax.all_gather(a, axis), part)  90.9 us
    add x5, other arithmetic, forward_compose(): later[0] * earlier[1] + later[1] * earlier[6]  87.3 us
  transfers between devices with their start and end apart: 11, of which 4 were waited for; matrix products, arithmetic and copies ran while one was open for 39% of the time, Pallas kernels for 0%

commit v1 on v0

v1 whole, which is shorter than its diff:
```python
import functools
import math

import jax
import jax.numpy as jnp
import ml_dtypes
import numpy as np
from jax import lax
from jax.experimental import pallas as pl
from jax.experimental.pallas import tpu as pltpu
from jax.sharding import PartitionSpec as P

GROUP = ("gx", "gz")
CHUNKS = 4
MIB = 1024 * 1024


def two_pieces(matrix):
    high = matrix.astype(ml_dtypes.bfloat16)
    low = (matrix - high.astype(np.float64)).astype(ml_dtypes.bfloat16)
    return high, low


def across_matrix(length):
    total = length // 2
    index = np.arange(total)
    signed = np.where(index < total // 2, index, index - total)
    angle = (signed[:, None] * np.arange(length)[None, :] % length) * (2.0 * math.pi / length)
    return np.concatenate([np.cos(angle), -np.sin(angle)]) / math.sqrt(length)


def along_matrix(length):
    numbers = np.arange(length // 4)
    angle = (numbers[:, None] * np.arange(length)[None, :] % length) * (2.0 * math.pi / length)
    return np.concatenate([np.cos(angle), -np.sin(angle)]) / math.sqrt(length)


def wave_square(along_first, along_local, along_total, across_total):
    along = (along_first + jnp.arange(along_local, dtype=jnp.int32)).astype(
        jnp.float32
    ) / along_total
    index = jnp.arange(across_total, dtype=jnp.int32)
    signed = jnp.where(index < across_total // 2, index, index - across_total)
    across = signed.astype(jnp.float32) / (across_total // 2)
    return along[:, None] * along[:, None] + across[None, :] * across[None, :]


def dot(a, b):
    return lax.dot_general(a, b, (((1,), (0,)), ((), ())), preferred_element_type=jnp.float32)


def dot_nt(a, b):
    return lax.dot_general(a, b, (((1,), (1,)), ((), ())), preferred_element_type=jnp.float32)


def transform_kernel(gx, gz, data, zh, zl, xh, xl, out, gh, gl):
    z_local, x_local = data.shape[2], data.shape[3]
    modes = zh.shape[0]
    half = modes // 2
    kx_total = xh.shape[0] // 2
    joint = out.shape[0]
    step = min(256, modes)
    for block in range(gx):
        for first in range(0, modes, step):
            total = None
            for side in range(gz):
                piece = data[block * gz + side, 0]
                cols = slice(side * z_local, (side + 1) * z_local)
                rows = slice(first, first + step)
                term = dot(zh[rows, cols], piece) + dot(zl[rows, cols], piece)
                total = term if total is None else total + term
            high = total.astype(jnp.bfloat16)
            place = slice(block * x_local, (block + 1) * x_local)
            gh[first : first + step, place] = high
            gl[first : first + step, place] = (total - high.astype(jnp.float32)).astype(
                jnp.bfloat16
            )
    tile = 128
    width = 256
    per_dest = out.shape[2]
    for first in range(0, kx_total, tile):
        for col in range(0, half, width):
            def product(base, mode):
                rows = slice(base, base + tile)
                cols = slice(mode, mode + width)
                return (
                    dot_nt(xh[rows], gh[cols])
                    + dot_nt(xh[rows], gl[cols])
                    + dot_nt(xl[rows], gh[cols])
                )

            real = product(first, col) - product(kx_total + first, half + col)
            imag = product(kx_total + first, col) + product(first, half + col)
            for part in range(0, tile, min(tile, per_dest)):
                size = min(tile, per_dest)
                dest, at = divmod(first + part, per_dest)
                out[dest, 0, at : at + size, col : col + width] = real[part : part + size]
                out[dest, 0, at : at + size, half + col : half + col + width] = imag[
                    part : part + size
                ]
    del joint


def transform(data, pieces, gx, gz):
    groups, rows, z_local, x_local = data.shape
    zh, zl, xh, xl = pieces
    modes = zh.shape[0]
    kx_total = xh.shape[0] // 2
    along_length = xh.shape[1]
    whole = lambda a: pl.BlockSpec(a.shape, lambda r: (0, 0), pipeline_mode=pl.Buffered(1))
    return pl.pallas_call(
        functools.partial(transform_kernel, gx, gz),
        grid=(rows,),
        in_specs=[
            pl.BlockSpec((groups, 1, z_local, x_local), lambda r: (0, r, 0, 0)),
            whole(zh), whole(zl), whole(xh), whole(xl),
        ],
        out_specs=pl.BlockSpec((groups, 1, kx_total // groups, modes), lambda r: (0, r, 0, 0)),
        out_shape=jax.ShapeDtypeStruct(
            (groups, rows, kx_total // groups, modes), jnp.float32
        ),
        scratch_shapes=[pltpu.VMEM((modes, along_length), jnp.bfloat16)] * 2,
        compiler_params=pltpu.CompilerParams(vmem_limit_bytes=56 * MIB),
        cost_estimate=pl.CostEstimate(
            flops=2 * rows * (2 * modes * along_length * gz * z_local
                              + 3 * 2 * kx_total * along_length * modes),
            bytes_accessed=data.size * 2 + 4 * rows * kx_total * modes,
            transcendentals=0,
        ),
        name="transform",
    )(data, zh, zl, xh, xl)


def spike_kernel(low, up, diag, curve, square, ip_ref, g_ref, h_ref, edge_ref):
    rows = ip_ref.shape[0]
    sq = square[...]
    zero = jnp.zeros_like(sq)

    def ahead(i, carry):
        ratio, spike = carry
        inverse = 1.0 / (diag[i] + curve[i] * sq - low[i] * ratio)
        spike = -low[i] * spike * inverse
        ip_ref[i] = inverse
        g_ref[i] = spike
        return up[i] * inverse, spike

    lax.fori_loop(0, rows, ahead, (zero, zero - 1.0), unroll=4)

    def back(n, carry):
        i = rows - 1 - n
        g_next, h_next = carry
        ratio = up[i] * ip_ref[i]
        g = g_ref[i] - ratio * g_next
        h = -ratio * h_next
        g_ref[i] = g
        h_ref[i] = h
        return g, h

    lax.fori_loop(0, rows, back, (zero, zero - 1.0), unroll=4)
    edge_ref[0] = g_ref[0]
    edge_ref[1] = g_ref[rows - 1]
    edge_ref[2] = h_ref[0]
    edge_ref[3] = h_ref[rows - 1]


def sweep_kernel(chunks, low, up, ip_ref, *refs):
    sources, (w_ref, edge_ref) = refs[:chunks], refs[chunks:]
    rows, width, modes = w_ref.shape
    half = modes // 2
    senders, per_chunk = sources[0].shape[0], sources[0].shape[1]
    per_sender = rows // senders
    zero = jnp.zeros((width, half), jnp.float32)

    def ahead(sender, carry):
        real, imag = carry
        for within in range(per_sender):
            i = sender * per_sender + within
            source = sources[within // per_chunk]
            inner = within % per_chunk
            inverse = ip_ref[i]
            real = (source[sender, inner, :, :half] - low[i] * real) * inverse
            imag = (source[sender, inner, :, half:] - low[i] * imag) * inverse
            w_ref[i, :, :half] = real
            w_ref[i, :, half:] = imag
        return real, imag

    lax.fori_loop(0, senders, ahead, (zero, zero))

    def back(n, carry):
        real, imag = carry
        i = rows - 1 - n
        ratio = up[i] * ip_ref[i]
        real = w_ref[i, :, :half] - ratio * real
        imag = w_ref[i, :, half:] - ratio * imag
        w_ref[i, :, :half] = real
        w_ref[i, :, half:] = imag
        return real, imag

    lax.fori_loop(0, rows, back, (zero, zero), unroll=8)
    edge_ref[0] = w_ref[0]
    edge_ref[1] = w_ref[rows - 1]


def finish_kernel(count, place, w_ref, g_ref, h_ref, edges, spikes, out):
    rows, width, modes = w_ref.shape
    half = modes // 2
    zero = jnp.zeros((width, half), jnp.float32)
    me = place[0]
    joined = []
    for side in range(2):
        cols = slice(side * half, (side + 1) * half)
        p, q = zero, zero
        kept = []
        for k in range(count):
            wa, wz = edges[k, 0, :, cols], edges[k, 1, :, cols]
            ga, gz, ha, hz = (spikes[k, n] for n in range(4))
            scale = 1.0 / (1.0 - ga * q)
            r = (wa - ga * p) * scale
            s = ha * scale
            p, q = wz - gz * p + gz * q * r, gz * q * s + hz
            kept.append((r, s, p, q))
        before, after = zero, zero
        following = zero
        for k in range(count - 1, -1, -1):
            r, s, p, q = kept[k]
            first = r - s * following
            last = p - q * following
            after = jnp.where(me == k - 1, first, after)
            before = jnp.where(me == k + 1, last, before)
            following = first
        joined.append((before, after))

    def one(i, carry):
        g, h = g_ref[i], h_ref[i]
        for side in range(2):
            cols = slice(side * half, (side + 1) * half)
            before, after = joined[side]
            out[0, i, :, cols] = w_ref[i, :, cols] - g * before - h * after
        return carry

    lax.fori_loop(0, rows, one, 0, unroll=4)


def local(pieces, fields, conductance, metric, section_shift, curvature, damping):
    row_count, z_local, x_local = fields.shape[1:]
    gx, gz, gy = (lax.axis_size(a) for a in ("gx", "gz", "gy"))
    groups = gx * gz
    my_group = lax.axis_index("gy")
    along_total = gx * x_local // 4
    along_local = along_total // groups
    across_total = gz * z_local // 2
    modes = 2 * across_total
    per_sender = row_count // groups
    chunks = min(CHUNKS, per_sender)
    per_chunk = per_sender // chunks

    raw = fields.reshape(groups, per_sender, z_local, x_local)
    sources = []
    for chunk in range(chunks):
        part = raw[:, chunk * per_chunk : (chunk + 1) * per_chunk]
        lines = lax.all_to_all(part, GROUP, split_axis=0, concat_axis=0)
        spectra = transform(lines, pieces, gx, gz)
        sources.append(lax.all_to_all(spectra, GROUP, split_axis=0, concat_axis=0))

    joint_index = lax.axis_index("gx") * gz + lax.axis_index("gz")
    square = wave_square(joint_index * along_local, along_local, along_total, across_total)
    nought = jnp.zeros((1,), jnp.float32)
    first_row = my_group * row_count
    metric_pad = jnp.concatenate([nought, metric, nought])
    metric_rows = lax.dynamic_slice_in_dim(metric_pad, first_row, row_count + 2)
    face_rows = lax.dynamic_slice_in_dim(conductance, first_row, row_count + 1)
    shift_rows = lax.dynamic_slice_in_dim(section_shift, first_row, row_count)
    curve_rows = lax.dynamic_slice_in_dim(curvature, first_row, row_count)
    low = -metric_rows[:row_count] * face_rows[:row_count]
    up = -metric_rows[2:] * face_rows[1:]
    diag = (
        metric_rows[1 : row_count + 1] * (face_rows[:row_count] + face_rows[1:])
        + shift_rows
        + damping[0]
    )
    smem = pl.BlockSpec(memory_space=pltpu.SMEM)
    params = pltpu.CompilerParams(vmem_limit_bytes=48 * MIB)

    block = min(16, along_local)
    row_shape = jax.ShapeDtypeStruct((row_count, along_local, across_total), jnp.float32)
    row_spec = pl.BlockSpec((row_count, block, across_total), lambda n: (0, n, 0))
    inverse, g_rows, h_rows, spikes = pl.pallas_call(
        spike_kernel,
        grid=(along_local // block,),
        in_specs=[smem] * 4 + [pl.BlockSpec((block, across_total), lambda n: (n, 0))],
        out_specs=[row_spec] * 3
        + [pl.BlockSpec((4, block, across_total), lambda n: (0, n, 0))],
        out_shape=[row_shape] * 3
        + [jax.ShapeDtypeStruct((4, along_local, across_total), jnp.float32)],
        compiler_params=params,
        cost_estimate=pl.CostEstimate(
            flops=12 * row_count * along_local * across_total,
            bytes_accessed=60 * MIB,
            transcendentals=0,
        ),
        name="spikes",
    )(low, up, diag, curve_rows, square)
    all_spikes = lax.all_gather(spikes, "gy")

    block = min(8, along_local)
    full_spec = pl.BlockSpec((row_count, block, modes), lambda n: (0, n, 0))
    half_spec = pl.BlockSpec((row_count, block, across_total), lambda n: (0, n, 0))
    swept, edges = pl.pallas_call(
        functools.partial(sweep_kernel, chunks),
        grid=(along_local // block,),
        in_specs=[smem] * 2
        + [half_spec]
        + [pl.BlockSpec((groups, per_chunk, block, modes), lambda n: (0, 0, n, 0))] * chunks,
        out_specs=[full_spec, pl.BlockSpec((2, block, modes), lambda n: (0, n, 0))],
        out_shape=[
            jax.ShapeDtypeStruct((row_count, along_local, modes), jnp.float32),
            jax.ShapeDtypeStruct((2, along_local, modes), jnp.float32),
        ],
        compiler_params=params,
        name="sweep",
    )(low, up, inverse, *sources)
    all_edges = lax.all_gather(edges, "gy")
    return pl.pallas_call(
        functools.partial(finish_kernel, gy),
        grid=(along_local // block,),
        in_specs=[
            smem, full_spec, half_spec, half_spec,
            pl.BlockSpec((gy, 2, block, modes), lambda n: (0, 0, n, 0)),
            pl.BlockSpec((gy, 4, block, across_total), lambda n: (0, 0, n, 0)),
        ],
        out_specs=pl.BlockSpec((1, row_count, block, modes), lambda n: (0, 0, n, 0)),
        out_shape=jax.ShapeDtypeStruct((1, row_count, along_local, modes), jnp.float32),
        compiler_params=params,
        name="finish",
    )(jnp.reshape(my_group, (1,)).astype(jnp.int32), swept, g_rows, h_rows, all_edges, all_spikes)


def solution(mesh):
    placed = (P(None, "gy", "gz", "gx"), P(), P(), P(), P(), P())

    def run(fields, *rest):
        pieces = two_pieces(across_matrix(fields.shape[2])) + two_pieces(
            along_matrix(fields.shape[3])
        )
        pieces = tuple(jnp.asarray(a) for a in pieces)
        return jax.shard_map(
            local,
            mesh=mesh,
            in_specs=((P(),) * 4,) + placed,
            out_specs=P(None, "gy", ("gx", "gz"), None),
            check_vma=False,
        )(pieces, fields, *rest)

    return run
```

time: 2500 us -> 891 us (0.36)
  other arithmetic: 1450 us -> 0.84 us
  Pallas kernels: 0 us -> 424 us
  waiting for transfers between devices: 421 us -> 92.3 us
  blocking collectives: 0 us -> 295 us
  matrix products: 248 us -> 0 us
  local copies, waits for them, and re-layouts: 237 us -> 22.7 us
  between operations: 98.6 us -> 14.6 us
    mul x10 -> x0, other arithmetic: 524 us -> none  [the longest x7 409 us: local(): local_map = tuple((entry * pivot_scale for entry in state))]
    pallas_call x0 -> x7, Pallas kernels: none -> 424 us  [the longest x4 379 us: transform(): pl.pallas_call(functools.partial(transform_kernel, gx, gz), grid=(rows,),...]
    all_to_all x0 -> x3, blocking collectives: none -> 295 us  [local(): lines = lax.all_to_all(part, GROUP, split_axis=0, concat_axis=0)]
    unnamed x44 -> x0, other arithmetic: 294 us -> none
    all_to_all x2 -> x5, waiting for transfers between devices: 328 us -> 46.1 us  [the longest x4 38.4 us: local(): sources.append(lax.all_to_all(spectra, GROUP, split_axis=0, concat_axis=0))]
    add x18 -> x2, other arithmetic: 266 us -> 0.16 us  [the longest x1 0.08 us: local(): metric_rows[1:row_count + 1] * (face_rows[:row_count] + face_rows[1:])]
    dot_general x10 -> x0, matrix products: 248 us -> none  [the longest x4 82.9 us: local(): jnp.einsum('czpn,pzk->cnk', zdata, jnp.stack([-sine, cosine]), precision=...]
    div x2 -> x0, other arithmetic: 179 us -> none  [the longest x1 138 us: local(): (source[:, current_row] - lower_band[current_row] * forward_swept) / pivots]
  transfers between devices with their start and end apart: 11 -> 7, of which waited for: 4 -> 3; matrix products, arithmetic and copies ran while one was open for 39% -> 0% of each run, Pallas kernels for 0% -> 47%
where the time goes in v1:
time: 891 us; the launch traced here: 874 us
  Pallas kernels  424 us (48%)
  blocking collectives  295 us (33%)
  waiting for transfers between devices  92.3 us (10%)
  starting transfers between devices  23.4 us (3%)
  local copies, waits for them, and re-layouts  22.7 us (3%)
  between operations  14.6 us (2%)
    pallas_call x4, Pallas kernels, transform(): pl.pallas_call(functools.partial(transform_kernel, gx, gz), grid=(rows,),...  379 us
    all_to_all x3, blocking collectives, local(): lines = lax.all_to_all(part, GROUP, split_axis=0, concat_axis=0)  295 us
    all_gather x1, waiting for transfers between devices, local(): all_edges = lax.all_gather(edges, 'gy')  46.2 us
    all_to_all x4, waiting for transfers between devices, local(): sources.append(lax.all_to_all(spectra, GROUP, split_axis=0, concat_axis=0))  38.4 us
    all_to_all x4, starting transfers between devices, local(): sources.append(lax.all_to_all(spectra, GROUP, split_axis=0, concat_axis=0))  18.2 us
    pallas_call x1, Pallas kernels, local(): pl.pallas_call(functools.partial(finish_kernel, gy), grid=(along_local //...  17.9 us
  transfers between devices with their start and end apart: 7, of which 3 were waited for; matrix products, arithmetic and copies ran while one was open for 0% of the time, Pallas kernels for 47%

profile of v1, /device:TPU:0, one launch (start us, length us, event | category | flops | bytes accessed | tf_op | source)
XLA Modules:
  0.0 873.9 jit_solution(12483111071711108672)
XLA Ops:
  6.5 17.5 %fusion.3 = (bf16[8,2,512,512]{3,2,1,0:T(8,128)(2,1)}, bf16[8,2,512,512]{3,2,1,0:T(8,128)(2,1)S(1)}, bf16[8,2,512,512]{3,2,1,0:T(8,128)(2,1)S(1)}, bf16[8,2,512,512]{3,2,1,0:T(8,128)(2,1)}) fusion(bf16[8,8,512,512]{3,2,1,0:T(8,128)(2,1)} %bitcast.8), kind=kLoop, calls=%fused_computation.10 | loop fusion | bytes 67108864 | tf_op jit(solution)/shard_map/slice | solution.py:260
  24.0 100.4 %all_to_all.40.data = bf16[8,2,512,512]{3,2,1,0:T(8,128)(2,1)} all-to-all(bf16[8,2,512,512]{3,2,1,0:T(8,128)(2,1)} %get-tuple-element.20), channel_id=1, replica_groups=mesh['gx'=4,'gz'=2,'gy'=4] {'gx','gz'}, dimensions={0} | all-to-all | bytes 16777216 | tf_op jit(solution)/shard_map/all_to_all | solution.py:261
  124.5 97.5 %all_to_all.41.data = bf16[8,2,512,512]{3,2,1,0:T(8,128)(2,1)} all-to-all(bf16[8,2,512,512]{3,2,1,0:T(8,128)(2,1)S(1)} %get-tuple-element.19), channel_id=1, replica_groups=mesh['gx'=4,'gz'=2,'gy'=4] {'gx','gz'}, dimensions={0} | all-to-all | bytes 16777216 | tf_op jit(solution)/shard_map/all_to_all | solution.py:261
  222.0 97.5 %all_to_all.42.data = bf16[8,2,512,512]{3,2,1,0:T(8,128)(2,1)} all-to-all(bf16[8,2,512,512]{3,2,1,0:T(8,128)(2,1)S(1)} %get-tuple-element.18), channel_id=1, replica_groups=mesh['gx'=4,'gz'=2,'gy'=4] {'gx','gz'}, dimensions={0} | all-to-all | bytes 16777216 | tf_op jit(solution)/shard_map/all_to_all | solution.py:261
  319.5 5.1 all-to-all-start.6
  325.3 1.3 dynamic_slice.13
  326.8 0.6 dynamic_slice.12
  327.4 0.6 fusion.2
  328.0 83.1 %transform.4 = f32[8,2,64,1024]{3,2,1,0:T(8,128)} custom-call(bf16[8,2,512,512]{3,2,1,0:T(8,128)(2,1)} %all_to_all.40.data, bf16[1024,1024]{1,0:T(8,128)(2,1)} %constant.44.clone.zh, bf16[1024,1024]{1,0:T(8,128)(2,1)} %constant.45.clone.zl, bf16[1024,2048]{1,0:T(8,128)(2,1)} %constant.46.clone.xh, bf16[1024,2048]{1,0:T(8,128)(2,1)} %constant.47.clone.xl), custom_call_target="tpu_custom_call" | custom-call | flops 42949672960 | bytes 12582912 | tf_op jit(solution)/shard_map/transform/pallas_call | solution.py:111
  411.1 7.6 all-to-all-done.6.data
  418.7 4.5 all-to-all-start.1
  423.3 98.6 %transform.5 = f32[8,2,64,1024]{3,2,1,0:T(8,128)} custom-call(bf16[8,2,512,512]{3,2,1,0:T(8,128)(2,1)} %all_to_all.41.data, bf16[1024,1024]{1,0:T(8,128)(2,1)} %constant.44.clone.zh, bf16[1024,1024]{1,0:T(8,128)(2,1)} %constant.45.clone.zl, bf16[1024,2048]{1,0:T(8,128)(2,1)} %constant.46.clone.xh, bf16[1024,2048]{1,0:T(8,128)(2,1)} %constant.47.clone.xl), custom_call_target="tpu_custom_call" | custom-call | flops 42949672960 | bytes 12582912 | tf_op jit(solution)/shard_map/transform/pallas_call | solution.py:111
  521.9 4.5 all-to-all-start.3
  526.4 98.6 %transform.6 = f32[8,2,64,1024]{3,2,1,0:T(8,128)} custom-call(bf16[8,2,512,512]{3,2,1,0:T(8,128)(2,1)} %all_to_all.42.data, bf16[1024,1024]{1,0:T(8,128)(2,1)} %constant.44.clone.zh, bf16[1024,1024]{1,0:T(8,128)(2,1)} %constant.45.clone.zl, bf16[1024,2048]{1,0:T(8,128)(2,1)} %constant.46.clone.xh, bf16[1024,2048]{1,0:T(8,128)(2,1)} %constant.47.clone.xl), custom_call_target="tpu_custom_call" | custom-call | flops 42949672960 | bytes 12582912 | tf_op jit(solution)/shard_map/transform/pallas_call | solution.py:111
  625.0 4.5 all-to-all-start.5
  629.5 99.0 %transform.7 = f32[8,2,64,1024]{3,2,1,0:T(8,128)} custom-call(bf16[8,2,512,512]{3,2,1,0:T(8,128)(2,1)} %all-to-all-done.6.data, bf16[1024,1024]{1,0:T(8,128)(2,1)} %constant.44.clone.zh, bf16[1024,1024]{1,0:T(8,128)(2,1)} %constant.45.clone.zl, bf16[1024,2048]{1,0:T(8,128)(2,1)} %constant.46.clone.xh, bf16[1024,2048]{1,0:T(8,128)(2,1)} %constant.47.clone.xl), custom_call_target="tpu_custom_call" | custom-call | flops 42949672960 | bytes 12582912 | tf_op jit(solution)/shard_map/transform/pallas_call | solution.py:111
  728.6 4.6 all-to-all-start.7
  733.4 10.4 %spikes.1 = (f32[64,64,512]{2,1,0:T(8,128)}, f32[64,64,512]{2,1,0:T(8,128)}, f32[64,64,512]{2,1,0:T(8,128)}, f32[4,64,512]{2,1,0:T(8,128)}) custom-call(f32[64]{0:T(128)S(1)} %get-tuple-element.23.low, f32[64]{0:T(128)S(1)} %get-tuple-element.22.up, f32[64]{0:T(128)S(1)} %get-tuple-element.21.diag, f32[64]{0:T(128)S(1)} %dynamic_slice.15.curve, ...), custom_call_target="tpu_custom_call" | custom-call | flops 25165824 | bytes 62914560 | tf_op jit(solution)/shard_map/spikes/pallas_call | solution.py:287
  743.8 38.4 %all-to-all-done.7.refs_3_ = f32[8,2,64,1024]{3,2,1,0:T(8,128)} async-done(((f32[8,2,64,1024]{3,2,1,0:T(8,128)}), f32[8,2,64,1024]{3,2,1,0:T(8,128)}, u32[]{:S(2)}, u32[]{:S(2)}) %all-to-all-start.7) | async-done | bytes 4194336 | tf_op jit(solution)/shard_map/all_to_all | solution.py:263
  782.3 17.0 %sweep.1 = (f32[64,64,1024]{2,1,0:T(8,128)}, f32[2,64,1024]{2,1,0:T(8,128)}) custom-call(f32[64]{0:T(128)S(1)} %get-tuple-element.23.low, f32[64]{0:T(128)S(1)} %get-tuple-element.22.up, f32[64,64,512]{2,1,0:T(8,128)} %get-tuple-element.11.ip_ref, f32[8,2,64,1024]{3,2,1,0:T(8,128)} %all-to-all-done.1.refs_0_, f32[8,2,64,1024]{3,2,1,0:T(8,128)} %all-to-all-done.3.refs_1_, ...), custom_call_target="tpu_custom_call" | custom-call | tf_op jit(solution)/shard_map/sweep/pallas_call | solution.py:308
  799.3 46.2 %all-gather.5.cloned.1.call-done = f32[8,64,1024]{2,1,0:T(8,128)} async-done(((f32[2,64,1024]{2,1,0:T(8,128)}), f32[8,64,1024]{2,1,0:T(8,128)}) %all-gather.5.cloned.1.call-update) | async-done | bytes 2097168 | tf_op jit(solution)/shard_map/all_gather | solution.py:322
  845.5 1.6 copy-done
  847.1 1.6 copy-done.1
  848.7 17.9 %finish.1 = f32[1,64,64,1024]{3,2,1,0:T(8,128)} custom-call(s32[1]{0:T(128)} %bitcast.place, f32[64,64,1024]{2,1,0:T(8,128)} %get-tuple-element.12.w_ref, f32[64,64,512]{2,1,0:T(8,128)} %get-tuple-element.13.g_ref, f32[64,64,512]{2,1,0:T(8,128)} %get-tuple-element.14.h_ref, f32[4,2,64,1024]{3,2,1,0:T(8,128)S(1)} %bitcast.7, f32[4,4,64,512]{3,2,1,0:T(8,128)S(1)} %bitcast.6), custom_call_target="tpu_custom_call" | custom-call | tf_op jit(solution)/shard_map/finish/pallas_call | solution.py:323
  (27 shorter events, 0.5 us)
Async XLA Ops:
  319.5 7.1 copy-start.5
  319.5 7.8 copy-start.7
  319.5 99.2 %all-to-all-start.6 = ((bf16[8,2,512,512]{3,2,1,0:T(8,128)(2,1)}), bf16[8,2,512,512]{3,2,1,0:T(8,128)(2,1)}, u32[]{:S(2)}, u32[]{:S(2)}) async-start(bf16[8,2,512,512]{3,2,1,0:T(8,128)(2,1)} %get-tuple-element.17), calls=%async_computation.6 | async-start | bytes 16777216 | tf_op jit(solution)/shard_map/all_to_all | solution.py:261
  418.7 103.1 %all-to-all-start.1 = ((f32[8,2,64,1024]{3,2,1,0:T(8,128)}), f32[8,2,64,1024]{3,2,1,0:T(8,128)}, u32[]{:S(2)}, u32[]{:S(2)}) async-start(f32[8,2,64,1024]{3,2,1,0:T(8,128)} %transform.4), calls=%async_computation.1 | async-start | bytes 8388608 | tf_op jit(solution)/shard_map/all_to_all | solution.py:263
  521.9 103.1 %all-to-all-start.3 = ((f32[8,2,64,1024]{3,2,1,0:T(8,128)}), f32[8,2,64,1024]{3,2,1,0:T(8,128)}, u32[]{:S(2)}, u32[]{:S(2)}) async-start(f32[8,2,64,1024]{3,2,1,0:T(8,128)} %transform.5), calls=%async_computation.3 | async-start | bytes 8388608 | tf_op jit(solution)/shard_map/all_to_all | solution.py:263
  625.0 103.6 %all-to-all-start.5 = ((f32[8,2,64,1024]{3,2,1,0:T(8,128)}), f32[8,2,64,1024]{3,2,1,0:T(8,128)}, u32[]{:S(2)}, u32[]{:S(2)}) async-start(f32[8,2,64,1024]{3,2,1,0:T(8,128)} %transform.6), calls=%async_computation.5 | async-start | bytes 8388608 | tf_op jit(solution)/shard_map/all_to_all | solution.py:263
  728.5 4.7 copy-start.3
  728.5 4.7 copy-start.4
  728.5 4.7 copy-start.6
  728.5 4.8 copy-start.2
  728.6 53.7 %all-to-all-start.7 = ((f32[8,2,64,1024]{3,2,1,0:T(8,128)}), f32[8,2,64,1024]{3,2,1,0:T(8,128)}, u32[]{:S(2)}, u32[]{:S(2)}) async-start(f32[8,2,64,1024]{3,2,1,0:T(8,128)} %transform.7), calls=%async_computation.7 | async-start | bytes 8388608 | tf_op jit(solution)/shard_map/all_to_all | solution.py:263
  733.1 66.2 %all-gather.7.cloned.1.call-start = ((), (), s32[]{:S(2)}) async-start(), calls=%async_computation.9 | async-start | bytes 2621440 | tf_op jit(solution)/shard_map/all_gather | solution.py:303
  743.8 101.7 %all-gather.5.cloned.1.call-start = ((), (), s32[]{:S(2)}) async-start(), calls=%async_computation.8 | async-start | bytes 2621440 | tf_op jit(solution)/shard_map/all_gather | solution.py:322
  845.5 1.6 copy-start
  847.1 1.6 copy-start.1
Sparse Core Ops, SparseCore 0:
  743.9 48.2 all-gather.6
  799.4 46.0 all-gather.4

commit v2 on v1

--- a/solution.py
+++ b/solution.py
@@ -255,11 +255,14 @@
     per_chunk = per_sender // chunks
 
     raw = fields.reshape(groups, per_sender, z_local, x_local)
-    sources = []
+    sources, done = [], []
     for chunk in range(chunks):
         part = raw[:, chunk * per_chunk : (chunk + 1) * per_chunk]
+        if chunk >= 2:
+            part, done[chunk - 2] = lax.optimization_barrier((part, done[chunk - 2]))
         lines = lax.all_to_all(part, GROUP, split_axis=0, concat_axis=0)
-        spectra = transform(lines, pieces, gx, gz)
+        done.append(transform(lines, pieces, gx, gz))
+    for spectra in done:
         sources.append(lax.all_to_all(spectra, GROUP, split_axis=0, concat_axis=0))
 
     joint_index = lax.axis_index("gx") * gz + lax.axis_index("gz")

time: 891 us -> 854 us (0.958)
  blocking collectives: 295 us -> 252 us
    all_to_all x3 -> x2, blocking collectives: 295 us -> 199 us  [local(): lines = lax.all_to_all(part, GROUP, split_axis=0, concat_axis=0)]
    all_to_all x0 -> x1, blocking collectives: none -> 53.5 us  [local(): sources.append(lax.all_to_all(spectra, GROUP, split_axis=0, concat_axis=0))]
    all_to_all x4 -> x3, starting transfers between devices: 18.2 us -> 13.6 us  [local(): sources.append(lax.all_to_all(spectra, GROUP, split_axis=0, concat_axis=0))]
    all_to_all x4 -> x3, waiting for transfers between devices: 38.4 us -> 38.5 us  [local(): sources.append(lax.all_to_all(spectra, GROUP, split_axis=0, concat_axis=0))]
  transfers between devices with their start and end apart: 7 -> 7, of which waited for: 3 -> 3; matrix products, arithmetic and copies ran while one was open for 0% -> 0% of each run, Pallas kernels for 47% -> 49%
where the time goes in v2:
time: 854 us; the launch traced here: 837 us
  Pallas kernels  424 us (50%)
  blocking collectives  252 us (30%)
  waiting for transfers between devices  95 us (11%)
  local copies, waits for them, and re-layouts  26.6 us (3%)
  starting transfers between devices  24 us (3%)
  between operations  14.5 us (2%)
    pallas_call x4, Pallas kernels, transform(): pl.pallas_call(functools.partial(transform_kernel, gx, gz), grid=(rows,),...  380 us
    all_to_all x2, blocking collectives, local(): lines = lax.all_to_all(part, GROUP, split_axis=0, concat_axis=0)  199 us
    all_to_all x1, blocking collectives, local(): sources.append(lax.all_to_all(spectra, GROUP, split_axis=0, concat_axis=0))  53.5 us
    all_gather x1, waiting for transfers between devices, local(): all_edges = lax.all_gather(edges, 'gy')  45.5 us
    all_to_all x3, waiting for transfers between devices, local(): sources.append(lax.all_to_all(spectra, GROUP, split_axis=0, concat_axis=0))  38.5 us
    slice x1, local copies, waits for them, and re-layouts, local(): part = raw[:, chunk * per_chunk:(chunk + 1) * per_chunk]  20.3 us
    pallas_call x1, Pallas kernels, local(): pl.pallas_call(functools.partial(finish_kernel, gy), grid=(along_local //...  17.9 us
  transfers between devices with their start and end apart: 7, of which 3 were waited for; matrix products, arithmetic and copies ran while one was open for 0% of the time, Pallas kernels for 49%

profile of v2, /device:TPU:0, one launch (start us, length us, event | category | flops | bytes accessed | tf_op | source)
XLA Modules:
  0.0 836.7 jit_solution(5063112719413695920)
XLA Ops:
  6.5 20.3 %fusion.3 = (bf16[8,2,512,512]{3,2,1,0:T(8,128)(2,1)S(1)}, bf16[8,2,512,512]{3,2,1,0:T(8,128)(2,1)}, bf16[8,2,512,512]{3,2,1,0:T(8,128)(2,1)}, bf16[8,2,512,512]{3,2,1,0:T(8,128)(2,1)}) fusion(bf16[8,8,512,512]{3,2,1,0:T(8,128)(2,1)} %bitcast.8), kind=kLoop, calls=%fused_computation.10 | loop fusion | bytes 67108864 | tf_op jit(solution)/shard_map/slice | solution.py:260
  26.9 99.1 %all_to_all.40.data = bf16[8,2,512,512]{3,2,1,0:T(8,128)(2,1)} all-to-all(bf16[8,2,512,512]{3,2,1,0:T(8,128)(2,1)S(1)} %get-tuple-element.25), channel_id=1, replica_groups=mesh['gx'=4,'gz'=2,'gy'=4] {'gx','gz'}, dimensions={0} | all-to-all | bytes 16777216 | tf_op jit(solution)/shard_map/all_to_all | solution.py:263
  125.9 5.1 all-to-all-start
  131.0 83.1 %transform.5 = f32[8,2,64,1024]{3,2,1,0:T(8,128)} custom-call(bf16[8,2,512,512]{3,2,1,0:T(8,128)(2,1)} %all_to_all.40.data, bf16[1024,1024]{1,0:T(8,128)(2,1)} %constant.44.clone.zh, bf16[1024,1024]{1,0:T(8,128)(2,1)} %constant.45.clone.zl, bf16[1024,2048]{1,0:T(8,128)(2,1)} %constant.46.clone.xh, bf16[1024,2048]{1,0:T(8,128)(2,1)} %constant.47.clone.xl), custom_call_target="tpu_custom_call" | custom-call | flops 42949672960 | bytes 12582912 | tf_op jit(solution)/shard_map/transform/pallas_call | solution.py:111
  214.0 11.0 %all-to-all-done.data = bf16[8,2,512,512]{3,2,1,0:T(8,128)(2,1)} async-done(((bf16[8,2,512,512]{3,2,1,0:T(8,128)(2,1)}), bf16[8,2,512,512]{3,2,1,0:T(8,128)(2,1)}, u32[]{:S(2)}, u32[]{:S(2)}) %all-to-all-start) | async-done | bytes 8388640 | tf_op jit(solution)/shard_map/all_to_all | solution.py:263
  225.1 4.5 all-to-all-start.3
  229.6 98.9 %transform.4 = f32[8,2,64,1024]{3,2,1,0:T(8,128)} custom-call(bf16[8,2,512,512]{3,2,1,0:T(8,128)(2,1)} %all-to-all-done.data, bf16[1024,1024]{1,0:T(8,128)(2,1)} %constant.44.clone.zh, bf16[1024,1024]{1,0:T(8,128)(2,1)} %constant.45.clone.zl, bf16[1024,2048]{1,0:T(8,128)(2,1)} %constant.46.clone.xh, bf16[1024,2048]{1,0:T(8,128)(2,1)} %constant.47.clone.xl), custom_call_target="tpu_custom_call" | custom-call | flops 42949672960 | bytes 12582912 | tf_op jit(solution)/shard_map/transform/pallas_call | solution.py:111
  328.5 53.5 %all_to_all.41.refs_0_ = f32[8,2,64,1024]{3,2,1,0:T(8,128)} all-to-all(f32[8,2,64,1024]{3,2,1,0:T(8,128)} %transform.4), channel_id=1, replica_groups=mesh['gx'=4,'gz'=2,'gy'=4] {'gx','gz'}, dimensions={0} | all-to-all | bytes 8388608 | tf_op jit(solution)/shard_map/all_to_all | solution.py:266
  382.0 99.7 %all_to_all.42.data = bf16[8,2,512,512]{3,2,1,0:T(8,128)(2,1)} all-to-all(bf16[8,2,512,512]{3,2,1,0:T(8,128)(2,1)} %get-tuple-element.19), channel_id=1, replica_groups=mesh['gx'=4,'gz'=2,'gy'=4] {'gx','gz'}, dimensions={0} | all-to-all | bytes 16777216 | tf_op jit(solution)/shard_map/all_to_all | solution.py:263
  481.7 5.2 all-to-all-start.4
  487.6 0.8 dynamic_slice.13
  488.6 98.6 %transform.7 = f32[8,2,64,1024]{3,2,1,0:T(8,128)} custom-call(bf16[8,2,512,512]{3,2,1,0:T(8,128)(2,1)} %all_to_all.42.data, bf16[1024,1024]{1,0:T(8,128)(2,1)} %constant.44.clone.zh, bf16[1024,1024]{1,0:T(8,128)(2,1)} %constant.45.clone.zl, bf16[1024,2048]{1,0:T(8,128)(2,1)} %constant.46.clone.xh, bf16[1024,2048]{1,0:T(8,128)(2,1)} %constant.47.clone.xl), custom_call_target="tpu_custom_call" | custom-call | flops 42949672960 | bytes 12582912 | tf_op jit(solution)/shard_map/transform/pallas_call | solution.py:111
  587.1 4.5 all-to-all-start.7
  591.7 99.0 %transform.6 = f32[8,2,64,1024]{3,2,1,0:T(8,128)} custom-call(bf16[8,2,512,512]{3,2,1,0:T(8,128)(2,1)} %all-to-all-done.4.data, bf16[1024,1024]{1,0:T(8,128)(2,1)} %constant.44.clone.zh, bf16[1024,1024]{1,0:T(8,128)(2,1)} %constant.45.clone.zl, bf16[1024,2048]{1,0:T(8,128)(2,1)} %constant.46.clone.xh, bf16[1024,2048]{1,0:T(8,128)(2,1)} %constant.47.clone.xl), custom_call_target="tpu_custom_call" | custom-call | flops 42949672960 | bytes 12582912 | tf_op jit(solution)/shard_map/transform/pallas_call | solution.py:111
  690.7 4.6 all-to-all-start.5
  695.4 0.1 add_add_fusion
  695.6 10.4 %spikes.1 = (f32[64,64,512]{2,1,0:T(8,128)}, f32[64,64,512]{2,1,0:T(8,128)}, f32[64,64,512]{2,1,0:T(8,128)}, f32[4,64,512]{2,1,0:T(8,128)}) custom-call(f32[64]{0:T(128)S(1)} %get-tuple-element.31.low, f32[64]{0:T(128)S(1)} %get-tuple-element.30.up, f32[64]{0:T(128)S(1)} %get-tuple-element.29.diag, f32[64]{0:T(128)S(1)} %dynamic_slice.15.curve, ...), custom_call_target="tpu_custom_call" | custom-call | flops 25165824 | bytes 62914560 | tf_op jit(solution)/shard_map/spikes/pallas_call | solution.py:290
  706.0 38.4 %all-to-all-done.5.refs_2_ = f32[8,2,64,1024]{3,2,1,0:T(8,128)} async-done(((f32[8,2,64,1024]{3,2,1,0:T(8,128)}), f32[8,2,64,1024]{3,2,1,0:T(8,128)}, u32[]{:S(2)}, u32[]{:S(2)}) %all-to-all-start.5) | async-done | bytes 4194336 | tf_op jit(solution)/shard_map/all_to_all | solution.py:266
  744.4 2.2 copy-done
  746.6 16.2 %sweep.1 = (f32[64,64,1024]{2,1,0:T(8,128)}, f32[2,64,1024]{2,1,0:T(8,128)}) custom-call(f32[64]{0:T(128)S(1)} %get-tuple-element.31.low, f32[64]{0:T(128)S(1)} %get-tuple-element.30.up, f32[64,64,512]{2,1,0:T(8,128)} %get-tuple-element.15.ip_ref, f32[8,2,64,1024]{3,2,1,0:T(8,128)S(1)} %copy-done, f32[8,2,64,1024]{3,2,1,0:T(8,128)} %all-to-all-done.3.refs_1_, ...), custom_call_target="tpu_custom_call" | custom-call | tf_op jit(solution)/shard_map/sweep/pallas_call | solution.py:311
  762.9 45.5 %all-gather.5.cloned.1.call-done = f32[8,64,1024]{2,1,0:T(8,128)} async-done(((f32[2,64,1024]{2,1,0:T(8,128)}), f32[8,64,1024]{2,1,0:T(8,128)}) %all-gather.5.cloned.1.call-update) | async-done | bytes 2097168 | tf_op jit(solution)/shard_map/all_gather | solution.py:325
  808.4 1.6 copy-done.1
  810.0 1.6 copy-done.2
  811.6 17.9 %finish.1 = f32[1,64,64,1024]{3,2,1,0:T(8,128)} custom-call(s32[1]{0:T(128)} %bitcast.place, f32[64,64,1024]{2,1,0:T(8,128)} %get-tuple-element.20.w_ref, f32[64,64,512]{2,1,0:T(8,128)} %get-tuple-element.21.g_ref, f32[64,64,512]{2,1,0:T(8,128)} %get-tuple-element.22.h_ref, f32[4,2,64,1024]{3,2,1,0:T(8,128)S(1)} %bitcast.7, f32[4,4,64,512]{3,2,1,0:T(8,128)S(1)} %bitcast.6), custom_call_target="tpu_custom_call" | custom-call | tf_op jit(solution)/shard_map/finish/pallas_call | solution.py:326
  (23 shorter events, 0.5 us)
Async XLA Ops:
  125.9 99.1 %all-to-all-start = ((bf16[8,2,512,512]{3,2,1,0:T(8,128)(2,1)}), bf16[8,2,512,512]{3,2,1,0:T(8,128)(2,1)}, u32[]{:S(2)}, u32[]{:S(2)}) async-start(bf16[8,2,512,512]{3,2,1,0:T(8,128)(2,1)} %get-tuple-element.27), calls=%async_computation | async-start | bytes 16777216 | tf_op jit(solution)/shard_map/all_to_all | solution.py:263
  225.1 103.4 %all-to-all-start.3 = ((f32[8,2,64,1024]{3,2,1,0:T(8,128)}), f32[8,2,64,1024]{3,2,1,0:T(8,128)}, u32[]{:S(2)}, u32[]{:S(2)}) async-start(f32[8,2,64,1024]{3,2,1,0:T(8,128)} %transform.5), calls=%async_computation.3 | async-start | bytes 8388608 | tf_op jit(solution)/shard_map/all_to_all | solution.py:266
  481.7 6.6 copy-start.3
  481.7 6.8 copy-start.5
  481.7 105.4 %all-to-all-start.4 = ((bf16[8,2,512,512]{3,2,1,0:T(8,128)(2,1)}), bf16[8,2,512,512]{3,2,1,0:T(8,128)(2,1)}, u32[]{:S(2)}, u32[]{:S(2)}) async-start(bf16[8,2,512,512]{3,2,1,0:T(8,128)(2,1)} %get-tuple-element.18), calls=%async_computation.4 | async-start | bytes 16777216 | tf_op jit(solution)/shard_map/all_to_all | solution.py:263
  587.1 103.6 %all-to-all-start.7 = ((f32[8,2,64,1024]{3,2,1,0:T(8,128)}), f32[8,2,64,1024]{3,2,1,0:T(8,128)}, u32[]{:S(2)}, u32[]{:S(2)}) async-start(f32[8,2,64,1024]{3,2,1,0:T(8,128)} %transform.7), calls=%async_computation.7 | async-start | bytes 8388608 | tf_op jit(solution)/shard_map/all_to_all | solution.py:266
  690.7 4.6 copy-start.4
  690.7 53.7 %all-to-all-start.5 = ((f32[8,2,64,1024]{3,2,1,0:T(8,128)}), f32[8,2,64,1024]{3,2,1,0:T(8,128)}, u32[]{:S(2)}, u32[]{:S(2)}) async-start(f32[8,2,64,1024]{3,2,1,0:T(8,128)} %transform.6), calls=%async_computation.5 | async-start | bytes 8388608 | tf_op jit(solution)/shard_map/all_to_all | solution.py:266
  695.3 67.6 %all-gather.7.cloned.1.call-start = ((), (), s32[]{:S(2)}) async-start(), calls=%async_computation.9 | async-start | bytes 2621440 | tf_op jit(solution)/shard_map/all_gather | solution.py:306
  705.9 102.4 %all-gather.5.cloned.1.call-start = ((), (), s32[]{:S(2)}) async-start(), calls=%async_computation.8 | async-start | bytes 2621440 | tf_op jit(solution)/shard_map/all_gather | solution.py:325
  744.4 2.2 copy-start
  808.4 1.6 copy-start.1
  810.0 1.6 copy-start.2
Sparse Core Ops, SparseCore 0:
  706.1 47.5 all-gather.6
  763.0 45.3 all-gather.4
